TPU v7x, 32 devices: a whole 2x2x4 slice. The times are simulated.
32 devices in a mesh: group: 8 (over z, x), mp: 4 (over y, core).
Axes of the slice: x: 2, y: 2, z: 4, core: 2. Of those that a mesh axis runs over, the one named last changes fastest.
Arguments:
- stream: bfloat16 [4096, 3584], P('group', 'mp'), may hold values from -6 to 6
- prenorm_gain: float32 [3584], replicated, may hold values from 0.25 to 12
- query_weight: bfloat16 [3584, 4096], P(None, 'mp'), may hold values from -0.09375 to 0.09375
- key_weight: bfloat16 [3584, 2048], P(None, 'mp'), may hold values from -0.09375 to 0.09375
- value_weight: bfloat16 [3584, 2048], P(None, 'mp'), may hold values from -0.09375 to 0.09375
- output_weight: bfloat16 [4096, 3584], P('mp'), may hold values from -0.09375 to 0.09375
- adapter_down_rows: bfloat16 [32, 16, 3584], P('group', None, 'mp'), may hold values from -0.09375 to 0.09375
- adapter_up_query: bfloat16 [32, 16, 4096], P('group', None, 'mp'), may hold values from -1.5 to 1.5
- request_adapter: int32 [8, 4], replicated, may hold values from 0 to 31
- adapter_row_index: int32 [32], replicated, may hold values from 0 to 31, each once
- request_token_length: int32 [8, 4], replicated, may hold values from 1 to 256, 512 in all within a row
- continues_previous: int32 [8], replicated, may hold values from 0 to 1, as said below
- request_cache_block: int32 [8, 4], replicated, may hold values from 0 to 15, as said below
- cached_length: int32 [8, 4], replicated, may hold values from 1 to 256
- cached_rotated_keys: bfloat16 [16, 256, 2048], P('group', None, 'mp'), may hold values from -6 to 6
- cached_value_rows: bfloat16 [16, 256, 2048], P('group', None, 'mp'), may hold values from -6 to 6
Outputs:
- attn_out: bfloat16 [4096, 3584], P('group', 'mp')
Inputs may be any that keep to these rules, and one draw needn't show every extreme that they name: `continues_previous`: the first group has 0; some group has 1. `request_cache_block`: the owner of block b is group b // 2; blocks may be shared by requests.
All inputs are finite; a program needn't handle non-finite values.
Results may differ from a plain program's by a relative error of at most 0.017.
The roundings to bfloat16 on the way count: a program that leaves them out, or rounds other values in their place, can miss the bound.
Values may be sent and summed in bfloat16 or wider, within the bound.
A program may use at most 128 MiB of HBM per device.

v0:
```python
import jax
import jax.numpy as jnp
from jax import lax
from jax.sharding import PartitionSpec as P

HEAD_WIDTH = 256
REQS = 4


adapter_scale = 2.0


def shifted(value, axis, steps):
    count = lax.axis_size(axis)
    first, last = (max(0, -steps), min(count, count - steps))
    return lax.ppermute(value, axis, [(source, source + steps) for source in range(first, last)])


def rotate(values, position, head_size):
    count = values.shape[0]
    shaped = values.reshape(count, -1, head_size)
    half = head_size // 2
    freq = 10000.0 ** (-jnp.arange(half, dtype=jnp.float32) / half)
    angle = position[:, None, None] * freq[None, None, :]
    cosine = jnp.cos(angle)
    sine = jnp.sin(angle)
    first = shaped[..., :half]
    second = shaped[..., half:]
    turned = jnp.concatenate(
        [first * cosine - second * sine, second * cosine + first * sine], axis=-1
    )
    return turned.reshape(count, -1)


def layout(lengths, cached, split_flag, prev_len, count):
    ends = jnp.cumsum(lengths)
    starts = ends - lengths
    place = jnp.arange(count, dtype=jnp.int32)
    member = ((place[:, None] >= starts[None, :]) & (place[:, None] < ends[None, :])).astype(
        jnp.int32
    )
    request = jnp.sum(member * jnp.arange(lengths.shape[0], dtype=jnp.int32)[None, :], axis=1)
    offset = place - jnp.sum(member * starts[None, :], axis=1)
    extra = jnp.where(request == 0, split_flag * prev_len, 0)
    position = jnp.sum(member * cached[None, :], axis=1) + extra + offset
    return (member, request, position.astype(jnp.float32))


def attend(
    query_vectors,
    keys,
    values,
    prev_keys,
    prev_values,
    cache_keys,
    cache_values,
    request,
    cached,
    split_flag,
    prev_len,
    head_size,
):
    count = query_vectors.shape[0]
    kv_heads = keys.shape[1] // head_size
    ratio = query_vectors.shape[1] // keys.shape[1]
    block = cache_keys.shape[1]
    slots = cache_keys.shape[0] * block
    every_key = jnp.concatenate([cache_keys.reshape(slots, -1), prev_keys, keys], 0).reshape(
        -1, kv_heads, head_size
    )
    every_value = jnp.concatenate(
        [cache_values.reshape(slots, -1), prev_values, values], 0
    ).reshape(-1, kv_heads, head_size)
    slot_req = jnp.arange(slots, dtype=jnp.int32) // block
    slot_col = jnp.arange(slots, dtype=jnp.int32) % block
    cache_ok = (request[:, None] == slot_req[None, :]) & (
        slot_col[None, :] < cached[slot_req][None, :]
    )
    place = jnp.arange(count, dtype=jnp.int32)
    prev_ok = (split_flag == 1) & (request[:, None] == 0) & (place[None, :] >= count - prev_len)
    own_ok = (request[:, None] == request[None, :]) & (place[None, :] <= place[:, None])
    allowed = jnp.concatenate([cache_ok, prev_ok, own_ok], 1)
    grouped = query_vectors.reshape(count, kv_heads, ratio, head_size)
    scores = jnp.einsum(
        "tkrd,skd->krts", grouped, every_key, preferred_element_type=jnp.float32
    ) * head_size ** (-0.5)
    scores = jnp.where(allowed[None, None], scores, jnp.float32(-1e30))
    top = jnp.max(scores, axis=-1, keepdims=True)
    weights = jnp.exp(scores - top)
    total = jnp.sum(weights, axis=-1)
    numer = jnp.einsum(
        "krts,skd->tkrd",
        weights.astype(jnp.bfloat16),
        every_value,
        preferred_element_type=jnp.float32,
    )
    result = numer / jnp.transpose(total, (2, 0, 1))[..., None]
    return result.reshape(count, -1).astype(jnp.bfloat16)


def on_device(
    stream,
    prenorm_gain,
    query_weight,
    key_weight,
    value_weight,
    output_weight,
    adapter_down_rows,
    adapter_up_query,
    request_adapter,
    adapter_row_index,
    request_token_length,
    continues_previous,
    request_cache_block,
    cached_length,
    cached_rotated_keys,
    cached_value_rows,
):
    count = stream.shape[0]
    width = stream.shape[1]
    group_at = lax.axis_index("group")
    model_at = lax.axis_index("mp")
    whole = lax.all_gather(stream, "mp", axis=1, tiled=True)
    wide = whole.astype(jnp.float32)
    normalized_input = (
        wide * lax.rsqrt(jnp.mean(wide * wide, axis=1, keepdims=True) + 1e-06) * prenorm_gain
    ).astype(jnp.bfloat16)
    normed_part = lax.dynamic_slice_in_dim(normalized_input, model_at * width, width, 1)
    before = jnp.maximum(group_at - 1, 0)
    lengths = request_token_length[group_at]
    cached = cached_length[group_at]
    split_flag = continues_previous[group_at]
    prev_len = request_token_length[before, REQS - 1]
    member, request, position = layout(lengths, cached, split_flag, prev_len, count)
    wanted = adapter_row_index[request_adapter[group_at]]
    pieces = (
        lax.all_gather(adapter_down_rows, "group", axis=0, tiled=True),
        lax.all_gather(adapter_up_query, "group", axis=0, tiled=True),
    )
    stored = jnp.arange(pieces[0].shape[0], dtype=jnp.int32)
    onehot = (wanted[:, None] == stored[None, :]).astype(jnp.bfloat16)
    new_down = jnp.einsum("rj,jkd->rkd", onehot, pieces[0], preferred_element_type=jnp.float32)
    new_up = jnp.einsum("rj,jkd->rkd", onehot, pieces[1], preferred_element_type=jnp.float32)
    chosen_down = new_down.astype(jnp.bfloat16)
    chosen_up = new_up.astype(jnp.bfloat16)
    rank_index = adapter_down_rows.shape[1]
    partial_low = jnp.einsum(
        "td,rkd->trk", normed_part, chosen_down, preferred_element_type=jnp.float32
    ).reshape(count, REQS * rank_index)
    low = lax.psum(partial_low, "mp").astype(jnp.bfloat16)
    own_columns = jnp.repeat(member, rank_index, axis=1).astype(jnp.bfloat16)
    query_update = jnp.dot(
        low * own_columns,
        chosen_up.reshape(REQS * rank_index, -1),
        preferred_element_type=jnp.float32,
    )
    query_vectors = (
        jnp.dot(normalized_input, query_weight, preferred_element_type=jnp.float32)
        + adapter_scale * query_update
    )
    query_vectors = rotate(query_vectors, position, HEAD_WIDTH).astype(jnp.bfloat16)
    keys = rotate(
        jnp.dot(normalized_input, key_weight, preferred_element_type=jnp.float32),
        position,
        HEAD_WIDTH,
    ).astype(jnp.bfloat16)
    values = jnp.dot(normalized_input, value_weight, preferred_element_type=jnp.float32).astype(
        jnp.bfloat16
    )
    prev_keys, prev_values = shifted((keys, values), "group", 1)
    blocks = request_cache_block[group_at]
    pieces = (
        lax.all_gather(cached_rotated_keys, "group", axis=0, tiled=True),
        lax.all_gather(cached_value_rows, "group", axis=0, tiled=True),
    )
    stored = jnp.arange(pieces[0].shape[0], dtype=jnp.int32)
    onehot = (blocks[:, None] == stored[None, :]).astype(jnp.bfloat16)
    new_keys = jnp.einsum("rj,jcd->rcd", onehot, pieces[0], preferred_element_type=jnp.float32)
    new_values = jnp.einsum("rj,jcd->rcd", onehot, pieces[1], preferred_element_type=jnp.float32)
    cache_keys = new_keys.astype(jnp.bfloat16)
    cache_values = new_values.astype(jnp.bfloat16)
    attended = attend(
        query_vectors,
        keys,
        values,
        prev_keys,
        prev_values,
        cache_keys,
        cache_values,
        request,
        cached,
        split_flag,
        prev_len,
        HEAD_WIDTH,
    )
    partial_out = jnp.dot(attended, output_weight, preferred_element_type=jnp.float32)
    return lax.psum_scatter(partial_out.astype(jnp.bfloat16), "mp", scatter_dimension=1, tiled=True)


def solution(mesh):
    placed = (
        P("group", "mp"),
        P(),
        P(None, "mp"),
        P(None, "mp"),
        P(None, "mp"),
        P("mp", None),
        P("group", None, "mp"),
        P("group", None, "mp"),
        P(),
        P(),
        P(),
        P(),
        P(),
        P(),
        P("group", None, "mp"),
        P("group", None, "mp"),
    )
    return jax.shard_map(
        on_device, mesh=mesh, in_specs=placed, out_specs=P("group", "mp"), check_vma=False
    )
```

profile of v0, /device:TPU:0, one launch (start us, length us, event | category | flops | bytes accessed | tf_op | source)
XLA Modules:
  0.0 335.9 jit_solution(6478019861982177569)
XLA Ops:
  6.5 0.7 all-gather.11.cloned.1.call-update
  7.3 0.7 all-gather.7.cloned.1.call-update
  8.1 0.7 all-gather.9.cloned.1.call-update
  9.4 1.3 constant_dynamic-slice_fusion.2
  11.3 1.2 dynamic_slice.24
  14.6 0.9 dynamic-slice_reduce_fusion
  15.7 0.9 fusion.64
  16.6 0.6 fusion.66
  17.2 2.5 compare_select_fusion.1
  20.1 35.8 %all_gather.18 = bf16[32,16,896]{2,1,0:T(8,128)(2,1)S(1)} all-gather(bf16[4,16,896]{2,1,0:T(8,128)(2,1)} %param.22), channel_id=1, replica_groups=mesh['group'=8,'mp'=4] {'group'}, dimensions={0}, use_global_device_ids=true | all-gather | bytes 1032192 | tf_op jit(solution)/shard_map/all_gather | solution.py:137
  55.9 1.3 gather_fusion
  57.4 0.8 compare_and_fusion
  58.3 1.0 multiply_cosine_fusion
  60.0 2.4 convolution_convert_fusion.2
  62.5 28.5 %all-gather.7.cloned.1.call-done = bf16[512,3584]{1,0:T(8,128)(2,1)} async-done(((bf16[512,896]{1,0:T(8,128)(2,1)}), bf16[512,3584]{1,0:T(8,128)(2,1)}) %all-gather.7.cloned.1.call-update) | async-done | bytes 3670032 | tf_op jit(solution)/shard_map/all_gather | solution.py:123
  91.0 3.0 fusion.6
  94.1 1.3 fusion.8
  95.4 0.6 copy-done.8
  96.0 2.9 convolution_convert_fusion.1
  98.9 4.2 %collective-permute-start = (bf16[512,512]{0,1:T(8,128)(2,1)}, bf16[512,512]{0,1:T(8,128)(2,1)}, u32[]{:S(2)}, u32[]{:S(2)}) collective-permute-start(bf16[512,512]{0,1:T(8,128)(2,1)} %convolution_convert_fusion.1), channel_id=1, source_target_pairs={{0,4},{4,8},{8,12},{12,16},{16,20},{20,24},{24,28},{1,5},{5,9},{9,... | collective-permute-start | bytes 1572872 | tf_op jit(solution)/shard_map/ppermute | solution.py:16
  103.5 2.1 fusion.67
  105.6 0.9 fusion.65
  106.7 1.2 copy.65
  108.2 1.1 copy.48
  109.2 3.4 %collective-permute-start.1 = (bf16[512,512]{0,1:T(8,128)(2,1)}, bf16[512,512]{0,1:T(8,128)(2,1)}, u32[]{:S(2)}, u32[]{:S(2)}) collective-permute-start(bf16[512,512]{0,1:T(8,128)(2,1)} %bitcast.17), channel_id=1, source_target_pairs={{0,4},{4,8},{8,12},{12,16},{16,20},{20,24},{24,28},{1,5},{5,9},{9,... | collective-permute-start | bytes 1572872 | tf_op jit(solution)/shard_map/ppermute | solution.py:16
  112.6 12.6 %all-reduce.1 = bf16[512,64]{0,1:T(8,128)(2,1)S(1)} all-reduce(f32[512,64]{0,1:T(8,128)S(1)} %bitcast.91), channel_id=1, replica_groups=mesh['group'=8,'mp'=4] {'mp'}, use_global_device_ids=true, to_apply=%region_5.6 | all-reduce | flops 32768 | bytes 196608 | tf_op jit(solution)/shard_map/psum | solution.py:150
  125.2 7.3 %fusion.68 = f32[512,1024]{1,0:T(8,128)S(1)} fusion(bf16[512,3584]{1,0:T(8,128)(2,1)} %copy-done.4, bf16[3584,1024]{1,0:T(8,128)(2,1)} %param.18), kind=kOutput, calls=%fused_computation.117 | convolution fusion | flops 3758096384 | bytes 13107200 | tf_op jit(solution)/shard_map/dot_general | solution.py:158
  132.6 1.8 multiply_add_fusion
  134.4 2.2 reshape.252
  136.6 1.6 subtract_convert_fusion
  138.1 0.6 pad_maximum_fusion
  138.7 1.1 copy.55
  139.8 2.1 copy.50
  141.9 39.7 %all-gather.9.cloned.1.call-done = bf16[16,256,512]{2,1,0:T(8,128)(2,1)} async-done(((bf16[2,256,512]{2,1,0:T(8,128)(2,1)}), bf16[16,256,512]{2,1,0:T(8,128)(2,1)}) %all-gather.9.cloned.1.call-update) | async-done | bytes 4194320 | tf_op jit(solution)/shard_map/all_gather | solution.py:173
  181.5 4.7 %fusion.28 = bf16[4,256,512]{2,0,1:T(4,128)(2,1)S(1)} fusion(bf16[16,256,512]{2,1,0:T(8,128)(2,1)} %all-gather.9.cloned.1.call-done, s32[4]{0:T(128)S(1)} %dynamic-slice_reduce_fusion.1), kind=kOutput, calls=%fused_computation.35 | convolution fusion | flops 17301568 | bytes 5242896 | tf_op jit(solution)/shard_map/rj,jcd->rcd/dot_general | solution.py:178
  186.7 1.1 copy.49
  187.9 5.9 %fusion.2 = (f32[2,2,512]{2,1,0:T(2,128)S(1)}, f32[2,2048,512,2]{2,1,3,0:T(8,128)S(1)}) fusion(pred[512,2048]{0,1:T(8,128)(4,1)S(1)} %pad_add_fusion, bf16[512,2,2,256]{3,0,2,1:T(8,128)(2,1)} %bitcast.87, bf16[512,2,256]{2,0,1:T(8,128)(2,1)} %copy-done.6, bf16[512,2,256]{2,0,1:T(8,128)(2,1)} %copy.50, bf16[1024,2,256]{2,0,1:T(8,128)(2,1)} %copy.49), kind=kOutput, calls=%fused_computation.5 | convolution fusion | flops 2166355968 | bytes 20979712 | tf_op jit(solution)/shard_map/tkrd,skd->krts/dot_general | solution.py:84
  193.8 5.7 %copy-done.2 = f32[2,2048,512,2]{2,1,3,0:T(8,128)} copy-done((f32[2,2048,512,2]{2,1,3,0:T(8,128)}, f32[2,2048,512,2]{2,1,3,0:T(8,128)S(1)}, u32[]{:S(2)}) %copy-start.2) | copy-done | bytes 16777240
  199.5 3.9 %fusion = f32[2,2,512]{2,1,0:T(2,128)S(1)} fusion(f32[2,2048,512,2]{2,1,3,0:T(8,128)S(1)} %get-tuple-element.25, f32[2,2,512]{2,1,0:T(2,128)S(1)} %get-tuple-element.24, pred[512,2048]{0,1:T(8,128)(4,1)S(1)} %pad_add_fusion), kind=kLoop, calls=%fused_computation.3 | loop fusion | flops 16775168 | bytes 17842176 | tf_op jit(solution)/shard_map/reduce_sum | solution.py:90
  203.4 51.8 %all-gather.5.cloned.1.call-done = bf16[16,256,512]{2,1,0:T(8,128)(2,1)} async-done(((bf16[2,256,512]{2,1,0:T(8,128)(2,1)}), bf16[16,256,512]{2,1,0:T(8,128)(2,1)}) %all-gather.5.cloned.1.call-update) | async-done | bytes 4194320 | tf_op jit(solution)/shard_map/all_gather | solution.py:174
  255.2 4.7 %fusion.25 = bf16[4,256,512]{2,0,1:T(4,128)(2,1)S(1)} fusion(bf16[16,256,512]{2,1,0:T(8,128)(2,1)} %all-gather.5.cloned.1.call-done, s32[4]{0:T(128)S(1)} %dynamic-slice_reduce_fusion.1), kind=kOutput, calls=%fused_computation.34 | convolution fusion | flops 17301568 | bytes 5242896 | tf_op jit(solution)/shard_map/rj,jcd->rcd/dot_general | solution.py:179
  259.9 1.2 copy.60
  261.2 0.8 reshape.302
  262.0 11.0 %fusion.22 = bf16[512,2,2,256]{0,3,2,1:T(8,128)(2,1)S(1)} fusion(f32[2,2048,512,2]{2,1,3,0:T(8,128)} %copy-done.2, f32[2,2,512]{2,1,0:T(2,128)S(1)} %get-tuple-element.24, pred[512,2048]{0,1:T(8,128)(4,1)S(1)} %pad_add_fusion, bf16[512,2,256]{0,2,1:T(8,128)(2,1)} %bitcast.2, bf16[512,2,256]{0,2,1:T(8,128)(2,1)} %bitcast.1, ...), kind=kOutput, calls=%fused_computation.31 | convolution fusion | flops 2171600896 | bytes 20987904 | tf_op jit(solution)/shard_map/krts,skd->tkrd/dot_general | solution.py:91
  273.0 8.6 %convolution_convert_fusion = bf16[512,3584]{1,0:T(8,128)(2,1)} fusion(bf16[512,1024]{0,1:T(8,128)(2,1)S(1)} %bitcast.97, bf16[1024,3584]{1,0:T(8,128)(2,1)} %param.21), kind=kOutput, calls=%fused_computation.13 | convolution fusion | flops 3759931392 | bytes 12058624 | tf_op jit(solution)/shard_map/dot_general | solution.py:196
  281.6 5.9 %copy.61 = bf16[512,3584]{0,1:T(8,128)(2,1)} copy(bf16[512,3584]{1,0:T(8,128)(2,1)} %convolution_convert_fusion) | data formatting | bytes 7340032
  287.5 39.7 %reduce-scatter.4.cloned.1.call-done = bf16[896,512]{1,0:T(8,128)(2,1)} async-done(((bf16[3584,512]{1,0:T(8,128)(2,1)}), bf16[896,512]{1,0:T(8,128)(2,1)}) %reduce-scatter.4.cloned.1.call-update) | async-done | bytes 917520
  327.2 2.2 copy.62
  (55 shorter events, 4.0 us)
Async XLA Ops:
  6.5 7.8 %copy-start = (s32[8,4]{0,1:T(4,128)S(1)}, s32[8,4]{0,1:T(4,128)}, u32[]{:S(2)}) copy-start(s32[8,4]{0,1:T(4,128)} %param.28) | copy-start | bytes 388
  6.5 53.4 %all-gather.11.cloned.1.call-start = ((), (), s32[]{:S(2)}) async-start(), calls=%async_computation.4 | async-start | bytes 1179648 | tf_op jit(solution)/shard_map/all_gather | solution.py:138
  7.3 83.7 %all-gather.7.cloned.1.call-start = ((), (), s32[]{:S(2)}) async-start(), calls=%async_computation.2 | async-start | bytes 4587520 | tf_op jit(solution)/shard_map/all_gather | solution.py:123
  8.0 173.5 %all-gather.9.cloned.1.call-start = ((), (), s32[]{:S(2)}) async-start(), calls=%async_computation.3 | async-start | bytes 4718592 | tf_op jit(solution)/shard_map/all_gather | solution.py:173
  8.7 246.5 %all-gather.5.cloned.1.call-start = ((), (), s32[]{:S(2)}) async-start(), calls=%async_computation.1 | async-start | bytes 4718592 | tf_op jit(solution)/shard_map/all_gather | solution.py:174
  9.3 317.9 %reduce-scatter.4.cloned.1.call-start = ((), (), s32[]{:S(2)}) async-start(), calls=%async_computation.5 | async-start | bytes 4587520
  59.2 48.7 %copy-start.5 = (f32[512,128]{1,0:T(8,128)}, f32[512,128]{1,0:T(8,128)S(1)}, u32[]{:S(2)}) copy-start(f32[512,128]{1,0:T(8,128)S(1)} %get-tuple-element.19) | copy-start | bytes 786436
  59.3 34.7 %copy-start.7 = (f32[3584]{0:T(1024)S(1)}, f32[3584]{0:T(1024)}, u32[]{:S(2)}) copy-start(f32[3584]{0:T(1024)} %param.17) | copy-start | bytes 43012
  91.0 3.1 copy-start.3
  93.9 2.1 copy-start.8
  96.0 7.5 %copy-start.4 = (bf16[512,3584]{1,0:T(8,128)(2,1)}, bf16[512,3584]{1,0:T(8,128)(2,1)S(1)}, u32[]{:S(2)}) copy-start(bf16[512,3584]{1,0:T(8,128)(2,1)S(1)} %fusion.8) | copy-start | bytes 11010052
  96.0 7.5 %copy-start.9 = (bf16[3584,512]{1,0:T(8,128)(2,1)S(1)}, bf16[3584,512]{1,0:T(8,128)(2,1)}, u32[]{:S(2)}) copy-start(bf16[3584,512]{1,0:T(8,128)(2,1)} %param.19) | copy-start | bytes 11010052
  98.9 163.0 %collective-permute-start = (bf16[512,512]{0,1:T(8,128)(2,1)}, bf16[512,512]{0,1:T(8,128)(2,1)}, u32[]{:S(2)}, u32[]{:S(2)}) collective-permute-start(bf16[512,512]{0,1:T(8,128)(2,1)} %convolution_convert_fusion.1), channel_id=1, source_target_pairs={{0,4},{4,8},{8,12},{12,16},{16,20},{20,24},{24,28},{1,5},{5,9},{9,... | collective-permute-start | bytes 1572872 | tf_op jit(solution)/shard_map/ppermute | solution.py:16
  108.2 24.4 %copy-start.6 = (bf16[512,2,256]{2,0,1:T(8,128)(2,1)}, bf16[512,2,256]{2,0,1:T(8,128)(2,1)S(1)}, u32[]{:S(2)}) copy-start(bf16[512,2,256]{2,0,1:T(8,128)(2,1)S(1)} %maximum_convert_fusion) | copy-start | bytes 1572868
  109.2 30.6 %collective-permute-start.1 = (bf16[512,512]{0,1:T(8,128)(2,1)}, bf16[512,512]{0,1:T(8,128)(2,1)}, u32[]{:S(2)}, u32[]{:S(2)}) collective-permute-start(bf16[512,512]{0,1:T(8,128)(2,1)} %bitcast.17), channel_id=1, source_target_pairs={{0,4},{4,8},{8,12},{12,16},{16,20},{20,24},{24,28},{1,5},{5,9},{9,... | collective-permute-start | bytes 1572872 | tf_op jit(solution)/shard_map/ppermute | solution.py:16
  193.8 5.7 %copy-start.2 = (f32[2,2048,512,2]{2,1,3,0:T(8,128)}, f32[2,2048,512,2]{2,1,3,0:T(8,128)S(1)}, u32[]{:S(2)}) copy-start(f32[2,2048,512,2]{2,1,3,0:T(8,128)S(1)} %get-tuple-element.25) | copy-start | bytes 50331652
  281.6 47.8 %copy-start.1 = (s32[8,4]{0,1:T(4,128)S(1)}, s32[8,4]{0,1:T(4,128)}, u32[]{:S(2)}) copy-start(s32[8,4]{0,1:T(4,128)} %param.28) | copy-start | bytes 388
Sparse Core Ops, SparseCore 0:
  9.5 49.3 all-gather.10
  60.4 30.4 all-gather.6
  93.1 88.3 all-gather.8
  183.5 71.6 all-gather.4
  287.6 39.4 reduce-scatter.3
where the time goes:
time: 337 us; the launch traced here: 336 us
  waiting for transfers between devices  162 us (48%)
  matrix products  52.1 us (15%)
  blocking collectives  48.4 us (14%)
  local copies, waits for them, and re-layouts  33.4 us (10%)
  other arithmetic  16 us (5%)
  between operations  16 us (5%)
  starting transfers between devices  7.73 us (2%)
    all_gather x1, waiting for transfers between devices, on_device(): lax.all_gather(cached_value_rows, 'group', axis=0, tiled=True)  51.8 us
    unnamed x6, waiting for transfers between devices  42.3 us
    all_gather x1, waiting for transfers between devices, on_device(): lax.all_gather(cached_rotated_keys, 'group', axis=0, tiled=True)  39.7 us
    all_gather x1, blocking collectives, on_device(): lax.all_gather(adapter_down_rows, 'group', axis=0, tiled=True)  35.8 us
    all_gather x1, waiting for transfers between devices, on_device(): whole = lax.all_gather(stream, 'mp', axis=1, tiled=True)  28.5 us
    unnamed x25, local copies, waits for them, and re-layouts  16.1 us
    psum x1, blocking collectives, on_device(): low = lax.psum(partial_low, 'mp').astype(jnp.bfloat16)  12.6 us
    dot_general x1, matrix products, attend(): jnp.einsum('krts,skd->tkrd', weights.astype(jnp.bfloat16), every_value, p...  11 us
  transfers between devices with their start and end apart: 7, of which 4 were waited for; matrix products, arithmetic and copies ran while one was open for 20% of the time, Pallas kernels for 0%

commit v1 on v0

v1 whole, which is shorter than its diff:
```python
import functools

import jax
import jax.numpy as jnp
from jax import lax
from jax.experimental import pallas as pl
from jax.experimental.pallas import tpu as pltpu
from jax.sharding import PartitionSpec as P

HEAD_WIDTH = 256
REQS = 4
ADAPTER_SCALE = 2.0
MESH = pl.DeviceIdType.MESH
F32 = jnp.float32
BF16 = jnp.bfloat16


def dot(a, b):
    return jnp.dot(a, b, preferred_element_type=F32)


def layout(lengths, cached, extra0, count):
    ends = jnp.cumsum(lengths)
    starts = ends - lengths
    place = jnp.arange(count, dtype=jnp.int32)
    member = (place[:, None] >= starts[None, :]) & (place[:, None] < ends[None, :])
    shift = cached - starts + jnp.where(jnp.arange(REQS) == 0, extra0, 0)
    position = place + jnp.sum(jnp.where(member, shift[None, :], 0), axis=1)
    return member, position.astype(F32)


def gather_kernel(
    G, M,
    ids, stream, gain, cosine, sine, own_columns, wq_in, wk_in, wv_in, down_in, up_in, ck_in, cv_in,
    q_out, k_out, v_out, pk_out, pv_out, gk, gv,
    parts, normed, wq, wk, wv, gd, gu, cd,
    local_sem, st_send, st_recv, fw_send, fw_recv, ring_send, ring_recv, cd_send, cd_recv,
    sh_send, sh_recv,
):
    g = lax.axis_index("group")
    m = lax.axis_index("mp")
    Y = M // 2
    half = G // 2
    y, c = m // 2, m % 2
    count = stream.shape[0]
    piece = count // 2
    width = stream.shape[1]
    partner = y * 2 + 1 - c

    def group_of(p):
        p = lax.rem(p + G, G)
        x = p // half
        z = p + x * (G - 1 - 2 * p)
        return 2 * z + x

    z, x = g // 2, g % 2
    place = z + x * (G - 1 - 2 * z)
    right, left = group_of(place + 1), group_of(place - 1)
    following, before = lax.rem(g + 1, G), lax.rem(g + G - 1, G)

    local = []
    for i, (src, dst) in enumerate(
        [(wk_in, wk), (wv_in, wv), (wq_in, wq), (down_in, gd.at[g]), (up_in, gu.at[g]),
         (ck_in, gk.at[g]), (cv_in, gv.at[g])]
    ):
        local.append(pltpu.make_async_copy(src, dst, local_sem.at[i]))
        local[-1].start()

    barrier = pltpu.get_barrier_semaphore()
    for d in range(1, M):
        pl.semaphore_signal(barrier, inc=1, device_id=(g, lax.rem(m + d, M)), device_id_type=MESH)
    for other in (right, left, following, before):
        pl.semaphore_signal(barrier, inc=1, device_id=(other, m), device_id_type=MESH)
    pl.semaphore_wait(barrier, M + 3)

    def rows_of(r):
        return pl.ds(r * piece, piece)

    def stream_send(d, r):
        to = partner if d == 0 else lax.rem(y + d, Y) * 2 + c
        return pltpu.make_async_remote_copy(
            src_ref=stream.at[rows_of(r)], dst_ref=parts.at[m, rows_of(r)],
            send_sem=st_send.at[d, r], recv_sem=st_recv.at[d, r],
            device_id=(g, to), device_id_type=MESH)

    def stream_got(d, r):
        owner = partner if d == 0 else lax.rem(y - d + Y, Y) * 2 + c
        return pltpu.make_async_remote_copy(
            src_ref=stream.at[rows_of(r)], dst_ref=parts.at[owner, rows_of(r)],
            send_sem=st_send.at[d, r], recv_sem=st_recv.at[d, r],
            device_id=(g, partner), device_id_type=MESH)

    def forward(d, r):
        owner = lax.rem(y - d + Y, Y) * 2 + c
        return pltpu.make_async_remote_copy(
            src_ref=parts.at[owner, rows_of(r)], dst_ref=parts.at[owner, rows_of(r)],
            send_sem=fw_send.at[d - 1, r], recv_sem=fw_recv.at[d - 1, r],
            device_id=(g, partner), device_id_type=MESH)

    def forwarded(d, r):
        owner = lax.rem(y - d + Y, Y) * 2 + 1 - c
        return pltpu.make_async_remote_copy(
            src_ref=parts.at[owner, rows_of(r)], dst_ref=parts.at[owner, rows_of(r)],
            send_sem=fw_send.at[d - 1, r], recv_sem=fw_recv.at[d - 1, r],
            device_id=(g, partner), device_id_type=MESH)

    held = (gd, gu, gk, gv)
    own = (down_in, up_in, ck_in, cv_in)

    def ring(a, way, s):
        sign = 1 if way == 0 else -1
        owner = group_of(place - sign * (s - 1))
        return pltpu.make_async_remote_copy(
            src_ref=own[a] if s == 1 else held[a].at[owner], dst_ref=held[a].at[owner],
            send_sem=ring_send.at[a, way, s - 1], recv_sem=ring_recv.at[a, way, s - 1],
            device_id=(right if way == 0 else left, m), device_id_type=MESH)

    def ring_got(a, way, s):
        sign = 1 if way == 0 else -1
        owner = group_of(place - sign * s)
        return pltpu.make_async_remote_copy(
            src_ref=own[a], dst_ref=held[a].at[owner],
            send_sem=ring_send.at[a, way, s - 1], recv_sem=ring_recv.at[a, way, s - 1],
            device_id=(right if way == 0 else left, m), device_id_type=MESH)

    def travels(a, way, s):
        return s < half or (s == half and a % 2 == way)

    def launch(arrays, s):
        for a in arrays:
            for way in range(2):
                if travels(a, way, s):
                    ring(a, way, s).start()

    def advance(arrays, s):
        for a in arrays:
            for way in range(2):
                if travels(a, way, s):
                    ring_got(a, way, s).wait_recv()
                if travels(a, way, s + 1):
                    ring(a, way, s + 1).start()

    order = (1, 0)
    launch((0, 1), 1)
    for r in order:
        for d in range(1, Y):
            stream_send(d, r).start()
        stream_send(0, r).start()
    parts[m] = stream[...]
    advance((0, 1), 1)
    launch((2, 3), 1)
    for s in range(2, half + 1):
        advance((0, 1), s)

    def norm(r):
        rows = rows_of(r)
        for d in range(1, Y):
            stream_got(d, r).wait_recv()
            forward(d, r).start()
        stream_got(0, r).wait_recv()
        for d in range(1, Y):
            forwarded(d, r).wait_recv()
        square = jnp.zeros((piece, 1), F32)
        for p in range(M):
            wide = parts[p, rows].astype(F32)
            square = square + jnp.sum(wide * wide, axis=1, keepdims=True)
        scale = lax.rsqrt(square / (M * width) + 1e-06)
        for p in range(M):
            normed[p, rows] = (parts[p, rows].astype(F32) * scale * gain[p]).astype(BF16)

    def project(r, weight, out, turn, low=None):
        rows = rows_of(r)

        @pl.loop(0, out.shape[1] // HEAD_WIDTH)
        def _(h):
            cols = pl.ds(pl.multiple_of(h * HEAD_WIDTH, HEAD_WIDTH), HEAD_WIDTH)
            total = dot(normed[0, rows], weight[0, :, cols])
            for p in range(1, M):
                total = total + dot(normed[p, rows], weight[p, :, cols])
            if low is not None:
                up = jnp.concatenate(
                    [gu[ids[i] // per, lax.rem(ids[i], per), :, cols] for i in range(REQS)], axis=0)
                total = total + ADAPTER_SCALE * dot(low, up)
            if turn:
                first, second = total[:, : HEAD_WIDTH // 2], total[:, HEAD_WIDTH // 2:]
                cs, sn = cosine[rows], sine[rows]
                total = jnp.concatenate(
                    [first * cs - second * sn, second * cs + first * sn], axis=1)
            out[rows, cols] = total.astype(BF16)

    per = gd.shape[1]
    last = pl.ds(count - piece, piece)

    def shift(i):
        src, dst = ((k_out, pk_out), (v_out, pv_out))[i]
        return pltpu.make_async_remote_copy(
            src_ref=src.at[last], dst_ref=dst, send_sem=sh_send.at[i], recv_sem=sh_recv.at[i],
            device_id=(following, m), device_id_type=MESH)

    local[3].wait()
    local[4].wait()
    for i in range(REQS):
        cd[m, i] = gd[ids[i] // per, lax.rem(ids[i], per)]

    def chosen(d):
        return pltpu.make_async_remote_copy(
            src_ref=cd.at[m], dst_ref=cd.at[m], send_sem=cd_send.at[d - 1],
            recv_sem=cd_recv.at[d - 1], device_id=(g, lax.rem(m + d, M)), device_id_type=MESH)

    def chosen_got(d):
        return pltpu.make_async_remote_copy(
            src_ref=cd.at[m], dst_ref=cd.at[lax.rem(m - d + M, M)], send_sem=cd_send.at[d - 1],
            recv_sem=cd_recv.at[d - 1], device_id=(g, lax.rem(m + d, M)), device_id_type=MESH)

    for d in range(1, M):
        chosen(d).start()

    norm(1)
    local[0].wait()
    project(1, wk, k_out, True)
    local[1].wait()
    project(1, wv, v_out, False)

    @pl.when(g < G - 1)
    def _():
        shift(0).start()
        shift(1).start()

    advance((2, 3), 1)
    norm(0)
    project(0, wk, k_out, True)
    project(0, wv, v_out, False)

    for d in range(1, M):
        chosen_got(d).wait_recv()
    local[2].wait()
    for r in order:
        low = jnp.zeros((piece, REQS * cd.shape[2]), F32)
        for p in range(M):
            factors = cd[p].reshape(REQS * cd.shape[2], width)
            low = low + lax.dot_general(
                normed[p, rows_of(r)], factors, (((1,), (1,)), ((), ())),
                preferred_element_type=F32)
        low = low.astype(BF16) * own_columns[rows_of(r)]
        project(r, wq, q_out, True, low)

    for s in range(2, half + 1):
        advance((2, 3), s)

    @pl.when(g > 0)
    def _():
        shift(0).wait_recv()
        shift(1).wait_recv()

    @pl.when(g == 0)
    def _():
        fill = [pltpu.make_async_copy(a.at[last], b, sh_recv.at[i])
                for i, (a, b) in enumerate(((k_out, pk_out), (v_out, pv_out)))]
        for one in fill:
            one.start()
        for one in fill:
            one.wait()

    @pl.when(g < G - 1)
    def _():
        shift(0).wait_send()
        shift(1).wait_send()

    for r in order:
        for d in range(Y):
            stream_send(d, r).wait_send()
        for d in range(1, Y):
            forward(d, r).wait_send()
    for a in range(4):
        for way in range(2):
            for s in range(1, half + 1):
                if travels(a, way, s):
                    ring(a, way, s).wait_send()
    for d in range(1, M):
        chosen(d).wait_send()
    local[5].wait()
    local[6].wait()


def attend_kernel(info, q, k, v, pk, pv, *rest):
    cache_k, cache_v, out = rest[:REQS], rest[REQS:2 * REQS], rest[2 * REQS]
    count = q.shape[0]
    tile = min(128, count)
    block = cache_k[0].shape[1]
    piece = pk.shape[0]
    ratio = q.shape[1] // HEAD_WIDTH
    starts, ends, cached = [], [], []
    run = jnp.int32(0)
    for r in range(REQS):
        starts.append(run)
        run = run + info[REQS + r]
        ends.append(run)
        cached.append(info[2 * REQS + r])
    flag, prev_len = info[3 * REQS], info[3 * REQS + 1]
    cut = jnp.where(flag == 1, piece - prev_len, piece)
    turned = (((1,), (1,)), ((), ()))
    for t in range(count // tile):
        rows = pl.ds(t * tile, tile)
        seen = (t + 1) * tile
        place = t * tile + lax.broadcasted_iota(jnp.int32, (tile, 1), 0)
        begin = jnp.zeros((tile, 1), jnp.int32)
        limit = []
        for r in range(REQS):
            mine = (place >= starts[r]) & (place < ends[r])
            begin = jnp.where(mine, starts[r], begin)
            limit.append(jnp.where(mine, cached[r], 0))
        from_prev = jnp.where(place < ends[0], cut, piece)
        col = lax.broadcasted_iota(jnp.int32, (tile, block), 1)
        col_prev = lax.broadcasted_iota(jnp.int32, (tile, piece), 1)
        col_own = lax.broadcasted_iota(jnp.int32, (tile, seen), 1)
        masks = [col < limit[r] for r in range(REQS)]
        masks.append(col_prev >= from_prev)
        masks.append((col_own >= begin) & (col_own <= place))
        keys = [cache_k[r][0] for r in range(REQS)] + [pk[...], k[:seen]]
        values = [cache_v[r][0] for r in range(REQS)] + [pv[...], v[:seen]]
        for h in range(ratio):
            cols = pl.ds(h * HEAD_WIDTH, HEAD_WIDTH)
            query = q[rows, cols]
            scores = [
                jnp.where(ok, lax.dot_general(query, key, turned, preferred_element_type=F32)
                          * HEAD_WIDTH ** -0.5, -1e30)
                for key, ok in zip(keys, masks)
            ]
            top = jnp.max(scores[0], axis=1, keepdims=True)
            for one in scores[1:]:
                top = jnp.maximum(top, jnp.max(one, axis=1, keepdims=True))
            total = jnp.zeros((tile, 1), F32)
            numer = jnp.zeros((tile, HEAD_WIDTH), F32)
            for one, value in zip(scores, values):
                weight = jnp.exp(one - top)
                total = total + jnp.sum(weight, axis=1, keepdims=True)
                numer = numer + dot(weight.astype(BF16), value)
            out[rows, cols] = (numer / total).astype(BF16)


def output_kernel(
    M, sliced, att, wo_in, out,
    wo, hold, mail, partner_in, post, post_in, own,
    local_sem, p_send, p_recv, y_send, y_recv,
):
    g = lax.axis_index("group")
    m = lax.axis_index("mp")
    Y = M // 2
    y, c = m // 2, m % 2
    partner = y * 2 + 1 - c
    width = out.shape[1]
    pieces = 2
    piece = out.shape[0] // pieces
    targets = [lax.rem(y + d, Y) * 2 + (c if e == 0 else 1 - c) for d in range(Y) for e in range(2)]
    loads = []
    for i, to in enumerate(targets):
        if sliced:
            src = wo_in.at[:, pl.ds(pl.multiple_of(to * width, 128), width)]
        else:
            src = wo_in.at[to]
        loads.append(pltpu.make_async_copy(src, wo.at[i], local_sem.at[i]))
    turn = [2 * d + e for d in list(range(1, Y)) + [0] for e in (1, 0)]
    for i in turn:
        loads[i].start()

    barrier = pltpu.get_barrier_semaphore()
    pl.semaphore_signal(barrier, inc=1, device_id=(g, partner), device_id_type=MESH)
    for d in range(1, Y):
        pl.semaphore_signal(
            barrier, inc=1, device_id=(g, lax.rem(y + d, Y) * 2 + c), device_id_type=MESH)
    pl.semaphore_wait(barrier, Y)

    def share(i, r):
        return dot(att[pl.ds(r * piece, piece)], wo[i])

    def to_partner(d, r):
        return pltpu.make_async_remote_copy(
            src_ref=mail.at[d, r], dst_ref=partner_in.at[d, r], send_sem=p_send.at[d, r],
            recv_sem=p_recv.at[d, r], device_id=(g, partner), device_id_type=MESH)

    def along(d, r):
        return pltpu.make_async_remote_copy(
            src_ref=post.at[d - 1, r], dst_ref=post_in.at[d - 1, r], send_sem=y_send.at[d - 1, r],
            recv_sem=y_recv.at[d - 1, r], device_id=(g, lax.rem(y + d, Y) * 2 + c),
            device_id_type=MESH)

    def give(d, r):
        mail[d, r] = share(2 * d + 1, r).astype(BF16)
        to_partner(d, r).start()

    def combine(d, r):
        to_partner(d, r).wait_recv()
        post[d - 1, r] = (hold[r] + partner_in[d, r].astype(F32)).astype(BF16)
        along(d, r).start()

    for d in range(1, Y):
        loads[2 * d + 1].wait()
        give(d, 0)
        loads[2 * d].wait()
        hold[0] = share(2 * d, 0)
        give(d, 1)
        combine(d, 0)
        hold[1] = share(2 * d, 1)
        combine(d, 1)
    loads[1].wait()
    give(0, 0)
    give(0, 1)
    loads[0].wait()
    for r in range(pieces):
        own[r] = share(0, r)
    for r in range(pieces):
        to_partner(0, r).wait_recv()
        total = own[r] + partner_in[0, r].astype(F32)
        for d in range(1, Y):
            along(d, r).wait_recv()
            total = total + post_in[d - 1, r].astype(F32)
        out[pl.ds(r * piece, piece)] = total.astype(BF16)
    for r in range(pieces):
        for d in range(Y):
            to_partner(d, r).wait_send()
        for d in range(1, Y):
            along(d, r).wait_send()


def on_device(
    G, M,
    stream, prenorm_gain, query_weight, key_weight, value_weight, output_weight,
    adapter_down_rows, adapter_up_query, request_adapter, adapter_row_index,
    request_token_length, continues_previous, request_cache_block, cached_length,
    cached_rotated_keys, cached_value_rows,
):
    count, width = stream.shape
    nq, nk = query_weight.shape[1], key_weight.shape[1]
    Y, half, piece = M // 2, G // 2, count // 2
    per, rank = adapter_down_rows.shape[:2]
    owned, block = cached_rotated_keys.shape[:2]
    group_at = lax.axis_index("group")
    before = jnp.maximum(group_at - 1, 0)
    lengths = request_token_length[group_at]
    cached = cached_length[group_at]
    flag = continues_previous[group_at]
    prev_len = request_token_length[before, REQS - 1]
    member, position = layout(lengths, cached, flag * prev_len, count)
    freq = 10000.0 ** (-jnp.arange(HEAD_WIDTH // 2, dtype=F32) / (HEAD_WIDTH // 2))
    angle = position[:, None] * freq[None, :]
    own_columns = jnp.repeat(member, rank, axis=1).astype(BF16)
    ids = adapter_row_index[request_adapter[group_at]]

    vmem, anywhere = pl.BlockSpec(memory_space=pltpu.VMEM), pl.BlockSpec(memory_space=pl.ANY)
    dma = pltpu.SemaphoreType.DMA
    flops = 2 * count * width * M * (nq + 2 * nk)
    q, k, v, pk, pv, gk, gv = pl.pallas_call(
        functools.partial(gather_kernel, G, M),
        out_shape=[
            jax.ShapeDtypeStruct((count, nq), BF16),
            jax.ShapeDtypeStruct((count, nk), BF16),
            jax.ShapeDtypeStruct((count, nk), BF16),
            jax.ShapeDtypeStruct((piece, nk), BF16),
            jax.ShapeDtypeStruct((piece, nk), BF16),
            jax.ShapeDtypeStruct((G, owned, block, nk), BF16),
            jax.ShapeDtypeStruct((G, owned, block, nk), BF16),
        ],
        in_specs=[pl.BlockSpec(memory_space=pltpu.SMEM)] + [vmem] * 5 + [anywhere] * 7,
        out_specs=[vmem] * 3 + [anywhere] * 4,
        scratch_shapes=[
            pltpu.VMEM((M, count, width), BF16),
            pltpu.VMEM((M, count, width), BF16),
            pltpu.VMEM((M, width, nq), BF16),
            pltpu.VMEM((M, width, nk), BF16),
            pltpu.VMEM((M, width, nk), BF16),
            pltpu.VMEM((G, per, rank, width), BF16),
            pltpu.VMEM((G, per, rank, nq), BF16),
            pltpu.VMEM((M, REQS, rank, width), BF16),
            dma((7,)), dma((Y, 2)), dma((Y, 2)), dma((Y - 1, 2)), dma((Y - 1, 2)),
            dma((4, 2, half)), dma((4, 2, half)), dma((M - 1,)), dma((M - 1,)), dma((2,)), dma((2,)),
        ],
        compiler_params=pltpu.CompilerParams(
            collective_id=0, has_side_effects=True, vmem_limit_bytes=48 * 2 ** 20),
        cost_estimate=pl.CostEstimate(flops=flops, bytes_accessed=32 * 2 ** 20, transcendentals=0),
        name="gather_project",
    )(
        ids, stream, prenorm_gain.reshape(M, 1, width), jnp.cos(angle), jnp.sin(angle), own_columns,
        query_weight.reshape(M, width, nq), key_weight.reshape(M, width, nk),
        value_weight.reshape(M, width, nk), adapter_down_rows, adapter_up_query,
        cached_rotated_keys, cached_value_rows,
    )

    info = jnp.concatenate(
        [request_cache_block[group_at], lengths, cached, flag[None], prev_len[None]])
    heads = nk // HEAD_WIDTH
    each = nq // heads

    def head(h, info):
        return (0, h)

    def picked(r):
        return pl.BlockSpec((1, block, HEAD_WIDTH), lambda h, info: (info[r], 0, h))

    blocks = [picked(r) for r in range(REQS)]
    own_kv = pl.BlockSpec((count, HEAD_WIDTH), head)
    prev_kv = pl.BlockSpec((piece, HEAD_WIDTH), head)
    every_k = gk.reshape(G * owned, block, nk)
    every_v = gv.reshape(G * owned, block, nk)
    attended = pl.pallas_call(
        attend_kernel,
        out_shape=jax.ShapeDtypeStruct((count, nq), BF16),
        grid_spec=pltpu.PrefetchScalarGridSpec(
            num_scalar_prefetch=1,
            grid=(heads,),
            in_specs=[pl.BlockSpec((count, each), head), own_kv, own_kv, prev_kv, prev_kv]
            + blocks + blocks,
            out_specs=pl.BlockSpec((count, each), head),
        ),
        compiler_params=pltpu.CompilerParams(vmem_limit_bytes=40 * 2 ** 20),
        name="attend",
    )(info, q, k, v, pk, pv, *([every_k] * REQS), *([every_v] * REQS))

    sliced = width % 128 == 0
    wo = output_weight
    if not sliced:
        wo = output_weight.reshape(nq, M, width).transpose(1, 0, 2)
    return pl.pallas_call(
        functools.partial(output_kernel, M, sliced),
        out_shape=jax.ShapeDtypeStruct((count, width), BF16),
        in_specs=[vmem, anywhere],
        out_specs=vmem,
        scratch_shapes=[
            pltpu.VMEM((M, nq, width), BF16),
            pltpu.VMEM((2, piece, width), F32),
            pltpu.VMEM((Y, 2, piece, width), BF16),
            pltpu.VMEM((Y, 2, piece, width), BF16),
            pltpu.VMEM((Y - 1, 2, piece, width), BF16),
            pltpu.VMEM((Y - 1, 2, piece, width), BF16),
            pltpu.VMEM((2, piece, width), F32),
            dma((M,)), dma((Y, 2)), dma((Y, 2)), dma((Y - 1, 2)), dma((Y - 1, 2)),
        ],
        compiler_params=pltpu.CompilerParams(
            collective_id=1, has_side_effects=True, vmem_limit_bytes=40 * 2 ** 20),
        name="project_out",
    )(attended, wo)


def solution(mesh):
    placed = (
        P("group", "mp"), P(), P(None, "mp"), P(None, "mp"), P(None, "mp"), P("mp", None),
        P("group", None, "mp"), P("group", None, "mp"), P(), P(), P(), P(), P(), P(),
        P("group", None, "mp"), P("group", None, "mp"),
    )
    return jax.shard_map(
        functools.partial(on_device, mesh.shape["group"], mesh.shape["mp"]),
        mesh=mesh, in_specs=placed, out_specs=P("group", "mp"), check_vma=False,
    )
```

time: 337 us -> 183 us (0.54)
  Pallas kernels: 0 us -> 162 us
  waiting for transfers between devices: 162 us -> 0 us
  matrix products: 52.1 us -> 0 us
  blocking collectives: 48.4 us -> 0 us
  local copies, waits for them, and re-layouts: 33.4 us -> 17.5 us
  between operations: 16 us -> 1.34 us
  other arithmetic: 16 us -> 1.36 us
  starting transfers between devices: 7.73 us -> 0 us
    pallas_call x0 -> x3, Pallas kernels: none -> 162 us  [the longest x1 124 us: on_device(): pl.pallas_call(functools.partial(gather_kernel, G, M), out_shape=[jax.Sha...]
    all_gather x4 -> x0, waiting for transfers between devices: 120 us -> none  [the longest x1 51.8 us: on_device(): lax.all_gather(cached_value_rows, 'group', axis=0, tiled=True)]
    dot_general x12 -> x0, matrix products: 52.1 us -> none  [the longest x1 11 us: attend(): jnp.einsum('krts,skd->tkrd', weights.astype(jnp.bfloat16), every_value, p...]
    unnamed x6 -> x0, waiting for transfers between devices: 42.3 us -> none
    all_gather x1 -> x0, blocking collectives: 35.8 us -> none  [on_device(): lax.all_gather(adapter_down_rows, 'group', axis=0, tiled=True)]
    psum x1 -> x0, blocking collectives: 12.6 us -> none  [on_device(): low = lax.psum(partial_low, 'mp').astype(jnp.bfloat16)]
    ppermute x2 -> x0, starting transfers between devices: 7.58 us -> none  [shifted(): lax.ppermute(value, axis, [(source, source + steps) for source in range(f...]
    reduce_sum x3 -> x1, other arithmetic: 6.95 us -> 0.09 us  [layout(): position = place + jnp.sum(jnp.where(member, shift[None, :], 0), axis=1)]
  transfers between devices with their start and end apart: 7 -> 0, of which waited for: 4 -> 0; matrix products, arithmetic and copies ran while one was open for 20% -> 0% of each run, Pallas kernels for 0% -> 0%
where the time goes in v1:
time: 183 us; the launch traced here: 182 us
  Pallas kernels  162 us (89%)
  local copies, waits for them, and re-layouts  17.5 us (10%)
    pallas_call x1, Pallas kernels, on_device(): pl.pallas_call(functools.partial(gather_kernel, G, M), out_shape=[jax.Sha...  124 us
    pallas_call x1, Pallas kernels, on_device(): pl.pallas_call(functools.partial(output_kernel, M, sliced), out_shape=jax...  27 us
    pallas_call x1, Pallas kernels, on_device(): pl.pallas_call(attend_kernel, out_shape=jax.ShapeDtypeStruct((count, nq),...  11.3 us
    unnamed x23, local copies, waits for them, and re-layouts  10.5 us

profile of v1, /device:TPU:0, one launch (start us, length us, event | category | flops | bytes accessed | tf_op | source)
XLA Modules:
  0.0 182.1 jit_solution(15798555305601073558)
XLA Ops:
  0.0 0.0 copy-start
  0.0 1.3 constant_dynamic-slice_fusion.2
  1.3 1.2 dynamic_slice.21
  3.7 0.9 dynamic-slice_reduce_fusion
  4.7 0.0 copy-done
  4.7 0.6 gather_fusion
  5.3 0.8 constant_dynamic-slice_fusion
  6.1 0.1 copy.23
  6.2 0.1 copy.22
  6.3 1.3 concatenate.3.info
  7.6 0.2 reduce-window.4
  7.8 0.1 select_reduce_fusion
  7.9 0.1 fusion.5
  7.9 0.7 reshape.82.gain
  8.7 0.1 copy.21.own_columns
  8.8 1.0 multiply_sine_fusion
  9.8 0.0 copy-start.3
  9.8 1.2 copy-done.3
  11.0 0.0 copy-start.4
  11.0 1.0 copy-done.4
  12.0 0.0 copy-start.5
  12.0 1.0 copy-done.5
  13.1 0.0 copy-start.6
  13.1 0.9 copy-done.6
  14.0 0.0 copy-start.7
  14.0 0.9 copy-done.7
  14.9 0.0 slice-start
  14.9 123.5 %gather_project.1 = (bf16[512,1024]{1,0:T(8,128)(2,1)S(1)}, bf16[512,512]{1,0:T(8,128)(2,1)S(1)}, bf16[512,512]{1,0:T(8,128)(2,1)S(1)}, bf16[256,512]{1,0:T(8,12...) custom-call(s32[4]{0:T(128)S(1)} %gather_fusion, ...), custom_call_target="tpu_custom_call" | custom-call | flops 7516192768 | bytes 33554432 | tf_op jit(solution)/shard_map/gather_project/pallas_call | solution.py:452
  138.4 0.0 copy-start.1
  138.4 2.2 %copy-done.1 = bf16[8,2,256,512]{3,2,1,0:T(8,128)(2,1)S(1)} copy-done((bf16[8,2,256,512]{3,2,1,0:T(8,128)(2,1)S(1)}, bf16[8,2,256,512]{3,2,1,0:T(8,128)(2,1)}, u32[]{:S(2)}) %copy-start.1) | copy-done | bytes 4194328
  140.6 0.0 copy-start.2
  140.6 2.2 %copy-done.2 = bf16[8,2,256,512]{3,2,1,0:T(8,128)(2,1)S(1)} copy-done((bf16[8,2,256,512]{3,2,1,0:T(8,128)(2,1)S(1)}, bf16[8,2,256,512]{3,2,1,0:T(8,128)(2,1)}, u32[]{:S(2)}) %copy-start.2) | copy-done | bytes 4194328
  142.8 0.0 slice-start.1
  142.8 11.3 %attend.1.att = bf16[512,1024]{1,0:T(8,128)(2,1)S(1)} custom-call(s32[14]{0:T(128)S(1)} %concatenate.3.info, bf16[512,1024]{1,0:T(8,128)(2,1)S(1)} %get-tuple-element.12.q, bf16[512,512]{1,0:T(8,128)(2,1)S(1)} %get-tuple-element.13.k, bf16[512,512]{1,0:T(8,128)(2,1)S(1)} %get-tuple-element.14.v, bf16[256,512]{1,0:T(8,128)(2,1)S(1)} %get-tuple-element.15.pk, ...), custom_call_target="tpu_custom_call" | custom-call | tf_op jit(solution)/shard_map/attend/pallas_call | solution.py:504
  154.1 0.0 slice-done
  154.1 0.0 slice-done.1
  154.1 27.0 %project_out.1 = bf16[512,896]{1,0:T(8,128)(2,1)S(1)} custom-call(bf16[512,1024]{1,0:T(8,128)(2,1)S(1)} %attend.1.att, bf16[1024,3584]{1,0:T(8,128)(2,1)S(1)} %bitcast.36), custom_call_target="tpu_custom_call" | custom-call | tf_op jit(solution)/shard_map/project_out/pallas_call | solution.py:522
  181.1 0.9 copy.25
  (7 shorter events, 0.0 us)
Async XLA Ops:
  0.0 4.7 %copy-start = (s32[32]{0:T(128)S(1)}, s32[32]{0:T(128)}, u32[]{:S(2)}) copy-start(s32[32]{0:T(128)} %param.25) | copy-start | bytes 388
  9.8 1.2 copy-start.3
  11.0 1.0 copy-start.4
  12.0 1.0 copy-start.5
  13.1 0.9 copy-start.6
  14.0 0.9 copy-start.7
  14.9 139.2 %slice-start = ((s8[7340032]{0:T(1024)(128)(4,1)}), s8[3145728]{0:T(1024)(128)(4,1)S(1)}, s32[]{:S(2)}) async-start(s8[7340032]{0:T(1024)(128)(4,1)} %bitcast.35), calls=%async_computation | async-start | bytes 6291456
  138.4 2.2 %copy-start.1 = (bf16[8,2,256,512]{3,2,1,0:T(8,128)(2,1)S(1)}, bf16[8,2,256,512]{3,2,1,0:T(8,128)(2,1)}, u32[]{:S(2)}) copy-start(bf16[8,2,256,512]{3,2,1,0:T(8,128)(2,1)} %get-tuple-element.17) | copy-start | bytes 12582916
  140.6 2.2 %copy-start.2 = (bf16[8,2,256,512]{3,2,1,0:T(8,128)(2,1)S(1)}, bf16[8,2,256,512]{3,2,1,0:T(8,128)(2,1)}, u32[]{:S(2)}) copy-start(bf16[8,2,256,512]{3,2,1,0:T(8,128)(2,1)} %get-tuple-element.18) | copy-start | bytes 12582916
  142.8 11.3 %slice-start.1 = ((s8[7340032]{0:T(1024)(128)(4,1)}), s8[4194304]{0:T(1024)(128)(4,1)S(1)}, s32[]{:S(2)}) async-start(s8[7340032]{0:T(1024)(128)(4,1)} %bitcast.35), calls=%async_computation.1 | async-start | bytes 8388608

commit v2 on v1

v2 whole, which is shorter than its diff:
```python
import functools

import jax
import jax.numpy as jnp
from jax import lax
from jax.experimental import pallas as pl
from jax.experimental.pallas import tpu as pltpu
from jax.sharding import PartitionSpec as P

HEAD_WIDTH = 256
REQS = 4
ADAPTER_SCALE = 2.0
MESH = pl.DeviceIdType.MESH
F32 = jnp.float32
BF16 = jnp.bfloat16


def dot(a, b):
    return jnp.dot(a, b, preferred_element_type=F32)


def layer_kernel(
    G, M, sliced,
    req_adapter, row_index, req_length, continues, req_block, req_cached,
    stream, gain, freq, wq_in, wk_in, wv_in, wo_in, down_in, up_in, ck_in, cv_in,
    out,
    q_out, k_out, v_out, pk_out, pv_out, gk, gv, cosine, sine, own_columns,
    parts, normed, wq, wk, wv, gd, gu, cd,
    acc, top, total_of, att, wo, hold, mail, partner_in, post, post_in, own_sum,
    local_sem, st_send, st_recv, fw_send, fw_recv, ring_send, ring_recv, cd_send, cd_recv,
    sh_send, sh_recv, wo_sem, p_send, p_recv, y_send, y_recv,
):
    g = lax.axis_index("group")
    m = lax.axis_index("mp")
    Y = M // 2
    half = G // 2
    y, c = m // 2, m % 2
    count = stream.shape[0]
    piece = count // 2
    width = stream.shape[1]
    partner = y * 2 + 1 - c

    def group_of(p):
        p = lax.rem(p + G, G)
        x = p // half
        z = p + x * (G - 1 - 2 * p)
        return 2 * z + x

    z, x = g // 2, g % 2
    place_in_ring = z + x * (G - 1 - 2 * z)
    right, left = group_of(place_in_ring + 1), group_of(place_in_ring - 1)
    following, before = lax.rem(g + 1, G), lax.rem(g + G - 1, G)

    local = []
    for i, (src, dst) in enumerate(
        [(wk_in, wk), (wv_in, wv), (wq_in, wq), (down_in, gd.at[g]), (up_in, gu.at[g]),
         (ck_in, gk.at[g]), (cv_in, gv.at[g])]
    ):
        local.append(pltpu.make_async_copy(src, dst, local_sem.at[i]))
        local[-1].start()
    targets = [lax.rem(y + d, Y) * 2 + (c if e == 0 else 1 - c) for d in range(Y) for e in range(2)]
    loads = []
    for i, to in enumerate(targets):
        if sliced:
            src = wo_in.at[:, pl.ds(pl.multiple_of(to * width, 128), width)]
        else:
            src = wo_in.at[to]
        loads.append(pltpu.make_async_copy(src, wo.at[i], wo_sem.at[i]))

    barrier = pltpu.get_barrier_semaphore()
    for d in range(1, M):
        pl.semaphore_signal(barrier, inc=1, device_id=(g, lax.rem(m + d, M)), device_id_type=MESH)
    for other in (right, left, following, before):
        pl.semaphore_signal(barrier, inc=1, device_id=(other, m), device_id_type=MESH)
    pl.semaphore_wait(barrier, M + 3)

    def rows_of(r):
        return pl.ds(r * piece, piece)

    def stream_send(d, r):
        to = partner if d == 0 else lax.rem(y + d, Y) * 2 + c
        return pltpu.make_async_remote_copy(
            src_ref=stream.at[rows_of(r)], dst_ref=parts.at[m, rows_of(r)],
            send_sem=st_send.at[d, r], recv_sem=st_recv.at[d, r],
            device_id=(g, to), device_id_type=MESH)

    def stream_got(d, r):
        owner = partner if d == 0 else lax.rem(y - d + Y, Y) * 2 + c
        return pltpu.make_async_remote_copy(
            src_ref=stream.at[rows_of(r)], dst_ref=parts.at[owner, rows_of(r)],
            send_sem=st_send.at[d, r], recv_sem=st_recv.at[d, r],
            device_id=(g, partner), device_id_type=MESH)

    def forward(d, r):
        owner = lax.rem(y - d + Y, Y) * 2 + c
        return pltpu.make_async_remote_copy(
            src_ref=parts.at[owner, rows_of(r)], dst_ref=parts.at[owner, rows_of(r)],
            send_sem=fw_send.at[d - 1, r], recv_sem=fw_recv.at[d - 1, r],
            device_id=(g, partner), device_id_type=MESH)

    def forwarded(d, r):
        owner = lax.rem(y - d + Y, Y) * 2 + 1 - c
        return pltpu.make_async_remote_copy(
            src_ref=parts.at[owner, rows_of(r)], dst_ref=parts.at[owner, rows_of(r)],
            send_sem=fw_send.at[d - 1, r], recv_sem=fw_recv.at[d - 1, r],
            device_id=(g, partner), device_id_type=MESH)

    held = (gd, gu, gk, gv)
    own = (down_in, up_in, ck_in, cv_in)

    def ring(a, way, s):
        sign = 1 if way == 0 else -1
        owner = group_of(place_in_ring - sign * (s - 1))
        return pltpu.make_async_remote_copy(
            src_ref=own[a] if s == 1 else held[a].at[owner], dst_ref=held[a].at[owner],
            send_sem=ring_send.at[a, way, s - 1], recv_sem=ring_recv.at[a, way, s - 1],
            device_id=(right if way == 0 else left, m), device_id_type=MESH)

    def ring_got(a, way, s):
        sign = 1 if way == 0 else -1
        owner = group_of(place_in_ring - sign * s)
        return pltpu.make_async_remote_copy(
            src_ref=own[a], dst_ref=held[a].at[owner],
            send_sem=ring_send.at[a, way, s - 1], recv_sem=ring_recv.at[a, way, s - 1],
            device_id=(right if way == 0 else left, m), device_id_type=MESH)

    def travels(a, way, s):
        return s < half or (s == half and a % 2 == way)

    def launch(arrays, s):
        for a in arrays:
            for way in range(2):
                if travels(a, way, s):
                    ring(a, way, s).start()

    def advance(arrays, s):
        for a in arrays:
            for way in range(2):
                if travels(a, way, s):
                    ring_got(a, way, s).wait_recv()
                if travels(a, way, s + 1):
                    ring(a, way, s + 1).start()

    order = (1, 0)
    launch((0, 1), 1)
    for r in order:
        for d in range(1, Y):
            stream_send(d, r).start()
        stream_send(0, r).start()
    launch((2,), 1)
    parts[m] = stream[...]
    for one in loads:
        one.start()

    lengths = [req_length[g, i] for i in range(REQS)]
    prev_len = req_length[jnp.maximum(g - 1, 0), REQS - 1]
    extra = jnp.where(continues[g] == 1, prev_len, 0)
    starts, ends = [], []
    run = jnp.int32(0)
    for i in range(REQS):
        starts.append(run)
        run = run + lengths[i]
        ends.append(run)

    def spread(rows, count, values, other):
        place = rows + lax.broadcasted_iota(jnp.int32, (count, 1), 0)
        result = jnp.full((count, 1), other, jnp.int32)
        for i in range(REQS):
            result = jnp.where((place >= starts[i]) & (place < ends[i]), values[i], result)
        return place, result

    cached = [req_cached[g, i] for i in range(REQS)]
    blocks = [req_block[g, i] for i in range(REQS)]
    ids = [row_index[req_adapter[g, i]] for i in range(REQS)]
    offsets = [cached[i] - starts[i] + (extra if i == 0 else 0) for i in range(REQS)]
    place, moved = spread(0, count, offsets, 0)
    angle = (place + moved).astype(F32) * freq[...]
    cosine[...] = jnp.cos(angle)
    sine[...] = jnp.sin(angle)
    rank = gd.shape[2]
    column = lax.broadcasted_iota(jnp.int32, (count, REQS * rank), 1)
    belongs = jnp.zeros((count, REQS * rank), F32)
    for i in range(REQS):
        mine = (place >= starts[i]) & (place < ends[i])
        mine = mine & (column >= i * rank) & (column < (i + 1) * rank)
        belongs = jnp.where(mine, 1.0, belongs)
    own_columns[...] = belongs.astype(BF16)

    advance((0, 1), 1)
    launch((3,), 1)

    def norm(r):
        rows = rows_of(r)
        for d in range(1, Y):
            stream_got(d, r).wait_recv()
            forward(d, r).start()
        stream_got(0, r).wait_recv()
        for d in range(1, Y):
            forwarded(d, r).wait_recv()
        square = jnp.zeros((piece, 1), F32)
        for p in range(M):
            wide = parts[p, rows].astype(F32)
            square = square + jnp.sum(wide * wide, axis=1, keepdims=True)
        scale = lax.rsqrt(square / (M * width) + 1e-06)
        for p in range(M):
            normed[p, rows] = (parts[p, rows].astype(F32) * scale * gain[:, p * width:(p + 1) * width]).astype(BF16)

    def project(r, weight, out, turn, low=None):
        rows = rows_of(r)

        @pl.loop(0, out.shape[1] // HEAD_WIDTH)
        def _(h):
            cols = pl.ds(pl.multiple_of(h * HEAD_WIDTH, HEAD_WIDTH), HEAD_WIDTH)
            total = dot(normed[0, rows], weight[0, :, cols])
            for p in range(1, M):
                total = total + dot(normed[p, rows], weight[p, :, cols])
            if low is not None:
                up = jnp.concatenate(
                    [gu[ids[i] // per, lax.rem(ids[i], per), :, cols] for i in range(REQS)], axis=0)
                total = total + ADAPTER_SCALE * dot(low, up)
            if turn:
                first, second = total[:, : HEAD_WIDTH // 2], total[:, HEAD_WIDTH // 2:]
                cs, sn = cosine[rows], sine[rows]
                total = jnp.concatenate(
                    [first * cs - second * sn, second * cs + first * sn], axis=1)
            out[rows, cols] = total.astype(BF16)

    per = gd.shape[1]
    last = pl.ds(count - piece, piece)

    def shift(i):
        src, dst = ((k_out, pk_out), (v_out, pv_out))[i]
        return pltpu.make_async_remote_copy(
            src_ref=src.at[last], dst_ref=dst, send_sem=sh_send.at[i], recv_sem=sh_recv.at[i],
            device_id=(following, m), device_id_type=MESH)

    def chosen(d):
        return pltpu.make_async_remote_copy(
            src_ref=cd.at[m], dst_ref=cd.at[m], send_sem=cd_send.at[d - 1],
            recv_sem=cd_recv.at[d - 1], device_id=(g, lax.rem(m + d, M)), device_id_type=MESH)

    def chosen_got(d):
        return pltpu.make_async_remote_copy(
            src_ref=cd.at[m], dst_ref=cd.at[lax.rem(m - d + M, M)], send_sem=cd_send.at[d - 1],
            recv_sem=cd_recv.at[d - 1], device_id=(g, lax.rem(m + d, M)), device_id_type=MESH)

    turned = (((1,), (1,)), ((), ()))
    heads = q_out.shape[1] // HEAD_WIDTH
    ratio = q_out.shape[1] // k_out.shape[1]

    def attend(r, keys_of, allowed, first=False):
        rows = rows_of(r)

        @pl.loop(0, heads)
        def _(h):
            cols = pl.ds(pl.multiple_of(h * HEAD_WIDTH, HEAD_WIDTH), HEAD_WIDTH)
            kv = pl.ds(pl.multiple_of(h // ratio * HEAD_WIDTH, HEAD_WIDTH), HEAD_WIDTH)
            keys, values = keys_of(kv)
            scores = lax.dot_general(
                q_out[rows, cols], keys, turned, preferred_element_type=F32) * HEAD_WIDTH ** -0.5
            scores = jnp.where(allowed, scores, -1e30)
            largest = jnp.max(scores, axis=1, keepdims=True)
            if not first:
                largest = jnp.maximum(largest, top[h, rows])
            weights = jnp.exp(scores - largest)
            total = jnp.sum(weights, axis=1, keepdims=True)
            numer = dot(weights.astype(BF16), values)
            if not first:
                fade = jnp.exp(top[h, rows] - largest)
                total = total + total_of[h, rows] * fade
                numer = numer + acc[rows, cols] * fade
            top[h, rows] = largest
            total_of[h, rows] = total
            acc[rows, cols] = numer

    def attend_own(r):
        seen = (r + 1) * piece
        at, begin = spread(r * piece, piece, starts, 0)
        col = lax.broadcasted_iota(jnp.int32, (piece, seen), 1)
        attend(r, lambda kv: (k_out[:seen, kv], v_out[:seen, kv]), (col >= begin) & (col <= at), True)

    def attend_prev(r):
        at, _ = spread(r * piece, piece, starts, 0)
        least = jnp.where(at < ends[0], piece - extra, piece)
        col = lax.broadcasted_iota(jnp.int32, (piece, piece), 1)
        attend(r, lambda kv: (pk_out[:, kv], pv_out[:, kv]), col >= least)

    owned, block = gk.shape[1], gk.shape[2]

    def attend_cache(r, owner):
        masks = []
        for i in range(owned):
            sees = [jnp.where(blocks[j] == owner * owned + i, cached[j], 0) for j in range(REQS)]
            _, limit = spread(r * piece, piece, sees, 0)
            masks.append(jnp.where(lax.broadcasted_iota(jnp.int32, (piece, block), 1) < limit, 1, 0))
        allowed = jnp.concatenate(masks, axis=1) > 0

        def keys_of(kv):
            return tuple(a[owner, :, :, kv].reshape(owned * block, HEAD_WIDTH) for a in (gk, gv))

        attend(r, keys_of, allowed)

    def finish(r):
        rows = rows_of(r)
        for h in range(heads):
            cols = pl.ds(h * HEAD_WIDTH, HEAD_WIDTH)
            att[rows, cols] = (acc[rows, cols] / total_of[h, rows]).astype(BF16)

    def share(i, r):
        return dot(att[rows_of(r)], wo[i])

    def to_partner(d, r):
        return pltpu.make_async_remote_copy(
            src_ref=mail.at[d, r], dst_ref=partner_in.at[d, r], send_sem=p_send.at[d, r],
            recv_sem=p_recv.at[d, r], device_id=(g, partner), device_id_type=MESH)

    def along(d, r):
        return pltpu.make_async_remote_copy(
            src_ref=post.at[d - 1, r], dst_ref=post_in.at[d - 1, r], send_sem=y_send.at[d - 1, r],
            recv_sem=y_recv.at[d - 1, r], device_id=(g, lax.rem(y + d, Y) * 2 + c),
            device_id_type=MESH)

    def give(d, r):
        mail[d, r] = share(2 * d + 1, r).astype(BF16)
        to_partner(d, r).start()

    def combine(d, r):
        to_partner(d, r).wait_recv()
        post[d - 1, r] = (hold[r] + partner_in[d, r].astype(F32)).astype(BF16)
        along(d, r).start()

    norm(1)
    local[0].wait()
    project(1, wk, k_out, True)
    local[1].wait()
    project(1, wv, v_out, False)

    @pl.when(g < G - 1)
    def _():
        shift(0).start()
        shift(1).start()

    advance((0, 1), 2)
    norm(0)
    project(0, wk, k_out, True)
    project(0, wv, v_out, False)
    advance((2,), 1)
    advance((0, 1), 3)
    advance((3,), 1)
    for s in range(4, half + 1):
        advance((0, 1), s)

    local[3].wait()
    local[4].wait()
    for i in range(REQS):
        cd[m, i] = gd[ids[i] // per, lax.rem(ids[i], per)]
    for d in range(1, M):
        chosen(d).start()
    for d in range(1, M):
        chosen_got(d).wait_recv()
    local[2].wait()
    for r in order:
        low = jnp.zeros((piece, REQS * rank), F32)
        for p in range(M):
            factors = cd[p].reshape(REQS * rank, width)
            low = low + lax.dot_general(
                normed[p, rows_of(r)], factors, turned, preferred_element_type=F32)
        low = low.astype(BF16) * own_columns[rows_of(r)]
        project(r, wq, q_out, True, low)

    for r in range(2):
        attend_own(r)
    advance((2, 3), 2)

    @pl.when(g > 0)
    def _():
        shift(0).wait_recv()
        shift(1).wait_recv()

    @pl.when(g == 0)
    def _():
        pk_out[...] = k_out[last]
        pv_out[...] = v_out[last]

    local[5].wait()
    local[6].wait()
    for r in range(2):
        attend_prev(r)
        attend_cache(r, g)
    for s in range(1, half):
        if s > 2:
            advance((2, 3), s)
        for sign in (-1, 1):
            for r in range(2):
                attend_cache(r, group_of(place_in_ring + sign * s))
    for one in loads:
        one.wait()
    advance((2, 3), half)
    for r in range(2):
        attend_cache(r, group_of(place_in_ring + half))
        finish(r)
        for d in range(1, Y):
            give(d, r)
            hold[r] = share(2 * d, r)
            combine(d, r)
    for r in range(2):
        give(0, r)
        own_sum[r] = share(0, r)
    for r in range(2):
        to_partner(0, r).wait_recv()
        total = own_sum[r] + partner_in[0, r].astype(F32)
        for d in range(1, Y):
            along(d, r).wait_recv()
            total = total + post_in[d - 1, r].astype(F32)
        out[rows_of(r)] = total.astype(BF16)

    @pl.when(g < G - 1)
    def _():
        shift(0).wait_send()
        shift(1).wait_send()

    for r in order:
        for d in range(Y):
            stream_send(d, r).wait_send()
            to_partner(d, r).wait_send()
        for d in range(1, Y):
            forward(d, r).wait_send()
            along(d, r).wait_send()
    for a in range(4):
        for way in range(2):
            for s in range(1, half + 1):
                if travels(a, way, s):
                    ring(a, way, s).wait_send()
    for d in range(1, M):
        chosen(d).wait_send()


def on_device(
    G, M,
    stream, prenorm_gain, query_weight, key_weight, value_weight, output_weight,
    adapter_down_rows, adapter_up_query, request_adapter, adapter_row_index,
    request_token_length, continues_previous, request_cache_block, cached_length,
    cached_rotated_keys, cached_value_rows,
):
    count, width = stream.shape
    nq, nk = query_weight.shape[1], key_weight.shape[1]
    Y, half, piece = M // 2, G // 2, count // 2
    per, rank = adapter_down_rows.shape[:2]
    owned, block = cached_rotated_keys.shape[:2]
    heads = nq // HEAD_WIDTH
    freq = 10000.0 ** (-jnp.arange(HEAD_WIDTH // 2, dtype=F32) / (HEAD_WIDTH // 2))
    sliced = width % 128 == 0
    wo = output_weight
    if not sliced:
        wo = output_weight.reshape(nq, M, width).transpose(1, 0, 2)

    smem, vmem = pl.BlockSpec(memory_space=pltpu.SMEM), pl.BlockSpec(memory_space=pltpu.VMEM)
    anywhere = pl.BlockSpec(memory_space=pl.ANY)
    dma = pltpu.SemaphoreType.DMA
    flops = 2 * count * width * M * (2 * nq + 2 * nk)
    return pl.pallas_call(
        functools.partial(layer_kernel, G, M, sliced),
        out_shape=jax.ShapeDtypeStruct((count, width), BF16),
        in_specs=[smem] * 6 + [vmem] * 3 + [anywhere] * 8,
        out_specs=vmem,
        scratch_shapes=[
            pltpu.VMEM((count, nq), BF16),
            pltpu.VMEM((count, nk), BF16),
            pltpu.VMEM((count, nk), BF16),
            pltpu.VMEM((piece, nk), BF16),
            pltpu.VMEM((piece, nk), BF16),
            pltpu.VMEM((G, owned, block, nk), BF16),
            pltpu.VMEM((G, owned, block, nk), BF16),
            pltpu.VMEM((count, HEAD_WIDTH // 2), F32),
            pltpu.VMEM((count, HEAD_WIDTH // 2), F32),
            pltpu.VMEM((count, REQS * rank), BF16),
            pltpu.VMEM((M, count, width), BF16),
            pltpu.VMEM((M, count, width), BF16),
            pltpu.VMEM((M, width, nq), BF16),
            pltpu.VMEM((M, width, nk), BF16),
            pltpu.VMEM((M, width, nk), BF16),
            pltpu.VMEM((G, per, rank, width), BF16),
            pltpu.VMEM((G, per, rank, nq), BF16),
            pltpu.VMEM((M, REQS, rank, width), BF16),
            pltpu.VMEM((count, nq), F32),
            pltpu.VMEM((heads, count, 1), F32),
            pltpu.VMEM((heads, count, 1), F32),
            pltpu.VMEM((count, nq), BF16),
            pltpu.VMEM((M, nq, width), BF16),
            pltpu.VMEM((2, piece, width), F32),
            pltpu.VMEM((Y, 2, piece, width), BF16),
            pltpu.VMEM((Y, 2, piece, width), BF16),
            pltpu.VMEM((Y - 1, 2, piece, width), BF16),
            pltpu.VMEM((Y - 1, 2, piece, width), BF16),
            pltpu.VMEM((2, piece, width), F32),
            dma((7,)), dma((Y, 2)), dma((Y, 2)), dma((Y - 1, 2)), dma((Y - 1, 2)),
            dma((4, 2, half)), dma((4, 2, half)), dma((M - 1,)), dma((M - 1,)), dma((2,)), dma((2,)),
            dma((M,)), dma((Y, 2)), dma((Y, 2)), dma((Y - 1, 2)), dma((Y - 1, 2)),
        ],
        compiler_params=pltpu.CompilerParams(
            collective_id=0, has_side_effects=True, vmem_limit_bytes=60 * 2 ** 20),
        cost_estimate=pl.CostEstimate(flops=flops, bytes_accessed=32 * 2 ** 20, transcendentals=0),
        name="layer",
    )(
        request_adapter, adapter_row_index, request_token_length, continues_previous,
        request_cache_block, cached_length,
        stream, prenorm_gain.reshape(1, M * width), freq[None, :],
        query_weight.reshape(M, width, nq), key_weight.reshape(M, width, nk),
        value_weight.reshape(M, width, nk), wo, adapter_down_rows, adapter_up_query,
        cached_rotated_keys, cached_value_rows,
    )


def solution(mesh):
    placed = (
        P("group", "mp"), P(), P(None, "mp"), P(None, "mp"), P(None, "mp"), P("mp", None),
        P("group", None, "mp"), P("group", None, "mp"), P(), P(), P(), P(), P(), P(),
        P("group", None, "mp"), P("group", None, "mp"),
    )
    return jax.shard_map(
        functools.partial(on_device, mesh.shape["group"], mesh.shape["mp"]),
        mesh=mesh, in_specs=placed, out_specs=P("group", "mp"), check_vma=False,
    )
```

time: 183 us -> 177 us (0.967)
  local copies, waits for them, and re-layouts: 17.5 us -> 8.87 us
  Pallas kernels: 162 us -> 167 us
    pallas_call x3 -> x1, Pallas kernels: 162 us -> 167 us  [on_device(): pl.pallas_call(functools.partial(layer_kernel, G, M, sliced), out_shape=j...]
    dynamic_slice x4 -> x0, local copies, waits for them, and re-layouts: 4.19 us -> none  [the longest x1 1.27 us: on_device(): prev_len = request_token_length[before, REQS - 1]]
    unnamed x23 -> x5, local copies, waits for them, and re-layouts: 10.5 us -> 7.54 us
where the time goes in v2:
time: 177 us
  Pallas kernels  167 us (94%)
  local copies, waits for them, and re-layouts  8.87 us (5%)
    pallas_call x1, Pallas kernels, on_device(): pl.pallas_call(functools.partial(layer_kernel, G, M, sliced), out_shape=j...  167 us
    unnamed x5, local copies, waits for them, and re-layouts  7.54 us

profile of v2, /device:TPU:0, one launch (start us, length us, event | category | flops | bytes accessed | tf_op | source)
XLA Modules:
  0.0 176.9 jit_solution(8999808448472770386)
XLA Ops:
  0.0 0.6 multiply_power_fusion.freq
  0.6 1.3 copy.17.req_adapter
  1.9 1.3 copy.18.req_length
  3.3 1.3 copy.19.req_block
  4.6 1.3 copy.20.req_cached
  6.0 1.3 reshape.25.gain
  7.3 167.4 %layer.1 = bf16[512,896]{1,0:T(8,128)(2,1)} custom-call(s32[8,4]{1,0:T(8,128)} %copy.17.req_adapter, s32[32]{0:T(128)} %row_index.1, s32[8,4]{1,0:T(8,128)} %copy.18.req_length, s32[8]{0:T(128)} %continues.1, s32[8,4]{1,0:T(8,128)} %copy.19.req_block, s32[8,4]{1,0:T(8,128)} %copy.20.req_cached, bf16[512,896]{1,0:T(8,128)(2,1)} %stream.1, ...), custom_call_target="tpu_custom_call" | custom-call | flops 11274289152 | bytes 33554432 | tf_op jit(solution)/shard_map/layer/pallas_call | solution.py:461
  174.7 2.2 %copy.22 = bf16[512,896]{1,0:T(8,128)(2,1)} copy(bf16[512,896]{1,0:T(8,128)(2,1)} %layer.1) | data formatting | bytes 1835008
